TPU v7x, 32 devices: a whole 2x2x4 slice. The times are simulated.
32 devices in a mesh: dp: 8 (over z, x), shard: 4 (over y, core).
Axes of the slice: x: 2, y: 2, z: 4, core: 2. Of those that a mesh axis runs over, the one named last changes fastest.
Arguments:
- gradient: bfloat16 [8, 2560, 2560], P(None, ('shard', 'dp')), may hold values from -1.5 to 1.5
- owner: int32 [8], replicated, may hold values from 0 to 7, each once
- a_inverse: bfloat16 [8, 2560, 2560], P('dp', 'shard'), as said below
- b_inverse: bfloat16 [8, 2560, 2560], P('dp', 'shard'), as said below
Outputs:
- preconditioned: bfloat16 [8, 2560, 2560], P(None, ('shard', 'dp'))
Inputs may be any that keep to these rules, and one draw needn't show every extreme that they name: owner names each of the 8 slots for exactly one layer. Every slot of a_inverse is a symmetric matrix. Every slot of b_inverse is a symmetric matrix.
All inputs are finite; a program needn't handle non-finite values.
Results may differ from a plain program's by a relative error of at most 0.0049.
Values may be sent and summed in bfloat16 or wider, within the bound.
A program may use at most 128 MiB of HBM per device.

v0:
```python
import jax
import jax.numpy as jnp
from jax import lax
from jax.sharding import PartitionSpec as P


def local(gradient, owner, a_inverse, b_inverse):
    layer_count = gradient.shape[0]
    chosen = (owner[:, None] == jnp.arange(layer_count, dtype=jnp.int32)[None, :]).astype(
        jnp.bfloat16
    )
    outgoing = jnp.einsum(
        "lo,lrc->orc", chosen, gradient, preferred_element_type=jnp.float32
    ).astype(jnp.bfloat16)
    owned = lax.all_to_all(outgoing, "dp", split_axis=0, concat_axis=1, tiled=True)
    grad_rows = owned[0]
    right_rows = b_inverse[0]
    left_rows = a_inverse[0]
    columns = grad_rows
    right_half = jnp.dot(
        columns,
        lax.all_gather(right_rows, "shard", axis=0, tiled=True),
        preferred_element_type=jnp.float32,
    ).astype(jnp.bfloat16)
    columns = left_rows
    summed = jnp.dot(
        columns,
        lax.all_gather(right_half, "shard", axis=0, tiled=True),
        preferred_element_type=jnp.float32,
    )
    result_rows = summed.astype(jnp.bfloat16)
    returned = lax.all_to_all(
        result_rows[None, :, :], "dp", split_axis=1, concat_axis=0, tiled=True
    )
    return jnp.take(returned, owner, axis=0)


def solution(mesh):
    in_specs = (P(None, ("shard", "dp"), None), P(), P("dp", "shard", None), P("dp", "shard", None))
    out_specs = P(None, ("shard", "dp"), None)
    return jax.shard_map(local, mesh=mesh, in_specs=in_specs, out_specs=out_specs, check_vma=False)
```

profile of v0, /device:TPU:0, one launch (start us, length us, event | category | flops | bytes accessed | tf_op | source)
XLA Modules:
  0.0 401.0 jit_solution(9742028505744985651)
XLA Ops:
  6.5 0.0 copy-start
  6.5 0.0 copy-start.2
  6.5 0.0 all-gather.6.cloned.1.call-start
  6.5 0.7 all-gather.6.cloned.1.call-update
  7.3 0.0 all-gather.4.cloned.1.call-start
  7.3 1.2 copy-done
  8.5 0.0 copy-done.2
  8.5 2.3 convolution_convert_fusion.1
  10.7 1.0 copy.10
  11.7 81.0 %all_to_all.21 = bf16[8,80,2560]{2,1,0:T(8,128)(2,1)} all-to-all(bf16[8,80,2560]{2,1,0:T(8,128)(2,1)S(1)} %copy.10), channel_id=1, replica_groups=mesh['dp'=8,'shard'=4] {'dp'}, dimensions={0} | all-to-all | bytes 6553600 | tf_op jit(solution)/shard_map/all_to_all | solution.py:15
  92.7 4.0 all-gather.6.cloned.1.call-done
  96.7 13.8 %fusion.2 = bf16[640,2560]{1,0:T(8,128)(2,1)} fusion(bf16[640,2560]{1,0:T(8,128)(2,1)} %bitcast.24, bf16[1,2560,2560]{2,1,0:T(8,128)(2,1)} %all-gather.6.cloned.1.call-done), kind=kOutput, calls=%fused_computation.3 | convolution fusion | flops 8390246400 | bytes 19660800 | tf_op jit(solution)/shard_map/dot_general | solution.py:20
  110.5 0.0 all-gather.4.cloned.1.call-update
  110.5 85.2 %all-gather.4.cloned.1.call-done = bf16[2560,2560]{1,0:T(8,128)(2,1)} async-done(((bf16[640,2560]{1,0:T(8,128)(2,1)}), bf16[2560,2560]{1,0:T(8,128)(2,1)}) %all-gather.4.cloned.1.call-update) | async-done | bytes 13107216 | tf_op jit(solution)/shard_map/all_gather | solution.py:28
  195.8 14.4 %fusion.5 = bf16[1,640,2560]{1,2,0:T(8,128)(2,1)S(1)} fusion(bf16[2560,2560]{1,0:T(8,128)(2,1)} %all-gather.4.cloned.1.call-done, bf16[1,640,2560]{2,1,0:T(8,128)(2,1)} %param.6), kind=kOutput, calls=%fused_computation.6 | convolution fusion | flops 8390246400 | bytes 19660800 | tf_op jit(solution)/shard_map/dot_general | solution.py:26
  210.2 10.2 %copy.11 = bf16[1,640,2560]{2,0,1:T(2,128)(2,1)} copy(bf16[1,640,2560]{1,2,0:T(8,128)(2,1)S(1)} %fusion.5) | data formatting | bytes 6553600 | tf_op jit(solution)/shard_map/broadcast_in_dim | solution.py:33
  220.4 0.5 broadcast.16
  220.9 70.0 %reduce = bf16[640,2560]{1,0:T(8,128)(2,1)S(1)} reduce(bf16[640,1,2560]{2,1,0:T(2,128)(2,1)} %bitcast.21, bf16[]{:T(256)} %broadcast.16), dimensions={1}, to_apply=%bitcast.17.reduce_sub_computation | reduce | bytes 6553602
  290.9 4.6 %reshape.24 = bf16[8,2,102400]{2,1,0:T(2,128)(2,1)} reshape(bf16[640,2560]{1,0:T(8,128)(2,1)S(1)} %reduce) | data formatting | bytes 6553600
  295.5 5.5 %all-to-all-start.1 = ((bf16[8,2,102400]{2,1,0:T(2,128)(2,1)}), bf16[8,2,102400]{2,1,0:T(2,128)(2,1)S(1)}, u32[]{:S(2)}, u32[]{:S(2)}) async-start(bf16[8,2,102400]{2,1,0:T(2,128)(2,1)} %reshape.24), calls=%async_computation.1 | async-start | bytes 6553600 | tf_op jit(solution)/shard_map/all_to_all | solution.py:32
  301.0 73.9 %all-to-all-done.1 = bf16[8,2,102400]{2,1,0:T(2,128)(2,1)S(1)} async-done(((bf16[8,2,102400]{2,1,0:T(2,128)(2,1)}), bf16[8,2,102400]{2,1,0:T(2,128)(2,1)S(1)}, u32[]{:S(2)}, u32[]{:S(2)}) %all-to-all-start.1) | async-done | bytes 3276832 | tf_op jit(solution)/shard_map/all_to_all | solution.py:32
  374.9 5.4 %reshape.25 = bf16[640,1,2560]{2,1,0:T(2,128)(2,1)} reshape(bf16[8,2,102400]{2,1,0:T(2,128)(2,1)S(1)} %all-to-all-done.1) | data formatting | bytes 6553600
  380.3 5.3 %copy.12 = bf16[1,640,2560]{2,1,0:T(8,128)(2,1)} copy(bf16[1,640,2560]{2,0,1:T(2,128)(2,1)} %bitcast.22) | data formatting | bytes 6553600
  385.6 0.0 copy-start.1
  385.6 4.5 %gather_fusion = bf16[8,80,2560]{2,1,0:T(8,128)(2,1)} fusion(bf16[8,80,2560]{2,1,0:T(8,128)(2,1)} %bitcast.23, s32[1024]{0:T(1024)S(1)} %pad_clamp_fusion), kind=kCustom, calls=%fused_computation | custom fusion | bytes 6553632 | tf_op jit(solution)/shard_map/jit(_take)/gather | solution.py:35
  390.1 4.0 %broadcast_select_fusion = bf16[8,80,2560]{2,1,0:T(8,128)(2,1)} fusion(bf16[8,80,2560]{2,1,0:T(8,128)(2,1)} %gather_fusion, pred[8]{0:T(512)(128)(4,1)S(1)} %compare_and_fusion), kind=kLoop, calls=%fused_computation.9 | loop fusion | flops 1638400 | bytes 6553608 | tf_op jit(solution)/shard_map/jit(_take)/select_n | solution.py:35
  394.2 0.0 copy-done.1
  (3 shorter events, 0.0 us)
Async XLA Ops:
  6.5 1.9 copy-start
  6.5 1.9 copy-start.2
  6.5 90.2 %all-gather.6.cloned.1.call-start = ((), (), s32[]{:S(2)}) async-start(), calls=%async_computation.3 | async-start | bytes 16384000 | tf_op jit(solution)/shard_map/all_gather | solution.py:22
  7.3 188.5 %all-gather.4.cloned.1.call-start = ((), (), s32[]{:S(2)}) async-start(), calls=%async_computation.2 | async-start | bytes 16384000 | tf_op jit(solution)/shard_map/all_gather | solution.py:28
  295.5 79.5 %all-to-all-start.1 = ((bf16[8,2,102400]{2,1,0:T(2,128)(2,1)}), bf16[8,2,102400]{2,1,0:T(2,128)(2,1)S(1)}, u32[]{:S(2)}, u32[]{:S(2)}) async-start(bf16[8,2,102400]{2,1,0:T(2,128)(2,1)} %reshape.24), calls=%async_computation.1 | async-start | bytes 6553600 | tf_op jit(solution)/shard_map/all_to_all | solution.py:32
  385.6 8.5 %copy-start.1 = (bf16[8,80,2560]{2,1,0:T(8,128)(2,1)S(1)}, bf16[8,80,2560]{2,1,0:T(8,128)(2,1)}, u32[]{:S(2)}) copy-start(bf16[8,80,2560]{2,1,0:T(8,128)(2,1)} %param.4) | copy-start | bytes 9830404
Sparse Core Ops, SparseCore 0:
  8.9 87.7 all-gather.5
  110.6 85.0 all-gather.3
where the time goes:
time: 401 us
  waiting for transfers between devices  164 us (41%)
  blocking collectives  81 us (20%)
  other arithmetic  74 us (18%)
  local copies, waits for them, and re-layouts  32.6 us (8%)
  matrix products  30.5 us (8%)
  between operations  13.5 us (3%)
  starting transfers between devices  5.55 us (1%)
    all_gather x1, waiting for transfers between devices, local(): lax.all_gather(right_half, 'shard', axis=0, tiled=True)  85.2 us
    all_to_all x1, blocking collectives, local(): lax.all_to_all(outgoing, 'dp', split_axis=0, concat_axis=1, tiled=True)  81 us
    all_to_all x1, waiting for transfers between devices, local(): lax.all_to_all(result_rows[None, :, :], 'dp', split_axis=1, concat_axis=0...  73.9 us
    unnamed x1, other arithmetic  70 us
    unnamed x10, local copies, waits for them, and re-layouts  16.9 us
    dot_general x1, matrix products, local(): jnp.dot(columns, lax.all_gather(right_half, 'shard', axis=0, tiled=True),...  14.4 us
    dot_general x1, matrix products, local(): jnp.dot(columns, lax.all_gather(right_rows, 'shard', axis=0, tiled=True),...  13.8 us
    broadcast_in_dim x1, local copies, waits for them, and re-layouts, local(): result_rows[None, :, :]  10.2 us
  transfers between devices with their start and end apart: 3, of which 3 were waited for; matrix products, arithmetic and copies ran while one was open for 1% of the time, Pallas kernels for 0%

commit v1 on v0

v1 whole, which is shorter than its diff:
```python
import functools
import jax
import jax.numpy as jnp
from jax import lax
from jax.experimental import pallas as pl
from jax.experimental.pallas import tpu as pltpu
from jax.sharding import PartitionSpec as P

MESH = pl.DeviceIdType.MESH
F32 = jnp.float32
BF16 = jnp.bfloat16


def general(gradient, owner, a_inverse, b_inverse):
    layer_count = gradient.shape[0]
    chosen = (owner[:, None] == jnp.arange(layer_count, dtype=jnp.int32)[None, :]).astype(BF16)
    outgoing = jnp.einsum("lo,lrc->orc", chosen, gradient, preferred_element_type=F32).astype(BF16)
    owned = lax.all_to_all(outgoing, "dp", split_axis=0, concat_axis=1, tiled=True)
    right_half = jnp.dot(
        owned[0],
        lax.all_gather(b_inverse[0], "shard", axis=0, tiled=True),
        preferred_element_type=F32,
    ).astype(BF16)
    result_rows = jnp.dot(
        a_inverse[0],
        lax.all_gather(right_half, "shard", axis=0, tiled=True),
        preferred_element_type=F32,
    ).astype(BF16)
    returned = lax.all_to_all(
        result_rows[None, :, :], "dp", split_axis=1, concat_axis=0, tiled=True
    )
    return jnp.take(returned, owner, axis=0)


def copy_block(owner_ref, in_ref, out_ref):
    out_ref[...] = in_ref[...]


def permute(owner, array, scatter):
    layers, rows, dim = array.shape
    plain = lambda l, owner_ref: (l, 0, 0)
    moved = lambda l, owner_ref: (owner_ref[l], 0, 0)
    return pl.pallas_call(
        copy_block,
        out_shape=jax.ShapeDtypeStruct(array.shape, array.dtype),
        grid_spec=pltpu.PrefetchScalarGridSpec(
            num_scalar_prefetch=1,
            grid=(layers,),
            in_specs=[pl.BlockSpec((1, rows, dim), plain if scatter else moved)],
            out_specs=pl.BlockSpec((1, rows, dim), moved if scatter else plain),
        ),
        cost_estimate=pl.CostEstimate(flops=0, bytes_accessed=4 * layers * rows * dim, transcendentals=0),
    )(owner, array)


def flip(index, mask):
    total, place = 0, 1
    while place <= mask:
        bit = lax.rem(index // place, 2)
        total = total + (1 - 2 * bit) * place if mask & place else total
        place *= 2
    return index + total


def dot(left, right):
    return jnp.dot(left, right, preferred_element_type=F32)


def kernel(
    groups, width, tile, side,
    g_ref, a_ref, b_ref, o_ref,
    gbuf, bfull, abuf, asib, ap, rbuf, psend, prec, obuf,
    local_sem, g_send, g_recv, b_send, b_recv, r_send, r_recv, p_send, p_recv, o_send, o_recv,
):
    _, rows, dim = g_ref.shape
    quarter, half = dim // 4, dim // 2
    d = lax.axis_index("dp")
    s = lax.axis_index("shard")
    y, c = s // 2, lax.rem(s, 2)
    sib = 2 * y + 1 - c
    across = 2 * (1 - y) + c
    across_sib = 2 * (1 - y) + 1 - c

    def rows_of(index, size, count=None):
        return pl.ds(pl.multiple_of(index * size, size), count or size)

    def remote(src, dst, send, recv, device):
        return pltpu.make_async_remote_copy(
            src_ref=src, dst_ref=dst, send_sem=send, recv_sem=recv, device_id=device, device_id_type=MESH
        )

    barrier = pltpu.get_barrier_semaphore()
    for k in range(1, groups):
        pl.semaphore_signal(barrier, inc=1, device_id=(flip(d, k), s), device_id_type=MESH)
    for other in (sib, across):
        pl.semaphore_signal(barrier, inc=1, device_id=(d, other), device_id_type=MESH)
    pl.semaphore_wait(barrier, groups + 1)

    g_copies = {}
    for k in (4, 5, 6, 7, 2, 3, 1):
        peer = flip(d, k)
        g_copies[k] = remote(
            g_ref.at[peer], gbuf.at[rows_of(d, rows)], g_send.at[k], g_recv.at[k], (peer, s)
        )
        g_copies[k].start()
    own_half = rows_of(y, half)
    other_half = rows_of(1 - y, half)
    b_across = remote(
        b_ref.at[:, own_half], bfull.at[rows_of(s, quarter), own_half], b_send.at[0], b_recv.at[0], (d, across)
    )
    b_across.start()
    b_sib = remote(b_ref, bfull.at[rows_of(s, quarter)], b_send.at[1], b_recv.at[1], (d, sib))
    b_sib.start()
    a_sib = remote(a_ref.at[:, rows_of(across_sib, quarter)], asib, b_send.at[2], b_recv.at[2], (d, sib))
    a_sib.start()
    a_own = pltpu.make_async_copy(a_ref, abuf, local_sem.at[0])
    a_own.start()
    b_own = pltpu.make_async_copy(b_ref, bfull.at[rows_of(s, quarter)], local_sem.at[1])
    b_own.start()
    g_own = pltpu.make_async_copy(g_ref.at[d], gbuf.at[rows_of(d, rows)], local_sem.at[2])
    g_own.start()

    a_own.wait()
    per = quarter // side

    def turn_own(i, carry):
        u, v = i // per, lax.rem(i, per)
        block = abuf[rows_of(u, side), pl.ds(pl.multiple_of(across * quarter + v * side, side), side)]
        ap[rows_of(v, side), pl.ds(pl.multiple_of(c * quarter + u * side, side), side)] = block.T
        return carry

    lax.fori_loop(0, per * per, turn_own, 0)
    a_sib.wait_recv()

    def turn_sib(i, carry):
        u, v = i // per, lax.rem(i, per)
        block = asib[rows_of(u, side), rows_of(v, side)]
        ap[rows_of(v, side), pl.ds(pl.multiple_of((1 - c) * quarter + u * side, side), side)] = block.T
        return carry

    lax.fori_loop(0, per * per, turn_sib, 0)

    b_own.wait()
    b_sib.wait_recv()
    wide = half // side

    def turn_b(i, carry):
        u, v = i // wide, lax.rem(i, wide)
        block = bfull[
            pl.ds(pl.multiple_of(y * half + u * side, side), side),
            pl.ds(pl.multiple_of((1 - y) * half + v * side, side), side),
        ]
        bfull[
            pl.ds(pl.multiple_of((1 - y) * half + v * side, side), side),
            pl.ds(pl.multiple_of(y * half + u * side, side), side),
        ] = block.T
        return carry

    lax.fori_loop(0, wide * wide, turn_b, 0)

    arrived = bfull.at[rows_of(across, quarter), other_half]
    remote(arrived, arrived, b_send.at[0], b_recv.at[0], (d, across)).wait_recv()
    relay = remote(arrived, arrived, b_send.at[3], b_recv.at[3], (d, sib))
    relay.start()
    relay.wait_recv()

    pair = 2 * rows
    r_copies = []
    for step in range(groups // 2):
        first = flip(d // 2, step)
        if step == 0:
            g_own.wait()
            g_copies[1].wait_recv()
        else:
            g_copies[2 * step].wait_recv()
            g_copies[2 * step + 1].wait_recv()
        here = pl.ds(pl.multiple_of(c * quarter + first * pair, pair), pair)

        def product(t, carry, first=first, here=here):
            columns = rows_of(t, tile)
            rbuf[here, columns] = dot(gbuf[rows_of(first, pair), :], bfull[:, columns]).astype(BF16)
            return carry

        lax.fori_loop(0, dim // tile, product, 0)
        copy = remote(rbuf.at[here], rbuf.at[here], r_send.at[step], r_recv.at[step], (d, sib))
        copy.start()
        r_copies.append(copy)
    for copy in r_copies:
        copy.wait_recv()

    chunks = dim // width

    def give(j, carry):
        psend[j] = dot(ap[...], rbuf[:, rows_of(j, width)]).astype(BF16)
        remote(psend.at[j], prec.at[j], p_send.at[j], p_recv.at[j], (d, across)).start()
        return carry

    lax.fori_loop(0, chunks, give, 0)

    def finish(j, carry):
        columns = rows_of(j, width)
        mine = dot(abuf[:, own_half], rbuf[:, columns])
        remote(psend.at[j], prec.at[j], p_send.at[j], p_recv.at[j], (d, across)).wait_recv()
        obuf[:, columns] = (mine + prec[j].astype(F32)).astype(BF16)
        for k in (4, 5, 6, 7, 2, 3, 1):
            peer = flip(d, k)
            remote(
                obuf.at[rows_of(peer, rows), columns], o_ref.at[d, :, columns],
                o_send.at[k], o_recv.at[k], (peer, s),
            ).start()
        return carry

    lax.fori_loop(0, chunks, finish, 0)
    o_own = pltpu.make_async_copy(obuf.at[rows_of(d, rows)], o_ref.at[d], local_sem.at[3])
    o_own.start()

    for k in range(1, groups):
        g_copies[k].wait_send()
    for copy in (b_across, b_sib, a_sib, relay, *r_copies):
        copy.wait_send()

    def sent(j, carry):
        remote(psend.at[j], prec.at[j], p_send.at[j], p_recv.at[j], (d, across)).wait_send()
        return carry

    lax.fori_loop(0, chunks, sent, 0)
    o_own.wait()
    for k in range(1, groups):
        peer = flip(d, k)
        whole = remote(obuf.at[rows_of(peer, rows)], o_ref.at[peer], o_send.at[k], o_recv.at[k], (peer, s))
        whole.wait_send()
        whole.wait_recv()


def fused(gradient, owner, a_inverse, b_inverse):
    groups, rows, dim = gradient.shape
    quarter, half = dim // 4, dim // 2
    width, tile, side = 256, 512, 128
    chunks = dim // width
    outgoing = permute(owner, gradient, True)
    anywhere = pl.BlockSpec(memory_space=pl.ANY)
    dma = pltpu.SemaphoreType.DMA
    returned = pl.pallas_call(
        functools.partial(kernel, groups, width, tile, side),
        out_shape=jax.ShapeDtypeStruct(gradient.shape, BF16),
        in_specs=[anywhere] * 3,
        out_specs=anywhere,
        scratch_shapes=[
            pltpu.VMEM((quarter, dim), BF16),
            pltpu.VMEM((dim, dim), BF16),
            pltpu.VMEM((quarter, dim), BF16),
            pltpu.VMEM((quarter, quarter), BF16),
            pltpu.VMEM((quarter, half), BF16),
            pltpu.VMEM((half, dim), BF16),
            pltpu.VMEM((chunks, quarter, width), BF16),
            pltpu.VMEM((chunks, quarter, width), BF16),
            pltpu.VMEM((quarter, dim), BF16),
            dma((4,)),
            dma((groups,)), dma((groups,)),
            dma((4,)), dma((4,)),
            dma((groups // 2,)), dma((groups // 2,)),
            dma((chunks,)), dma((chunks,)),
            dma((groups,)), dma((groups,)),
        ],
        compiler_params=pltpu.CompilerParams(
            collective_id=0, has_side_effects=True, vmem_limit_bytes=56 * 1024 * 1024
        ),
        cost_estimate=pl.CostEstimate(
            flops=4 * quarter * dim * dim, bytes_accessed=8 * quarter * dim, transcendentals=0
        ),
    )(outgoing, a_inverse[0], b_inverse[0])
    return permute(owner, returned, False)


def solution(mesh):
    in_specs = (P(None, ("shard", "dp"), None), P(), P("dp", "shard", None), P("dp", "shard", None))
    out_specs = P(None, ("shard", "dp"), None)

    def program(gradient, owner, a_inverse, b_inverse):
        dim = gradient.shape[1]
        fits = mesh.shape["dp"] == 8 and mesh.shape["shard"] == 4 and dim % 512 == 0
        local = fused if fits and (dim // 32) % 16 == 0 else general
        return jax.shard_map(local, mesh=mesh, in_specs=in_specs, out_specs=out_specs, check_vma=False)(
            gradient, owner, a_inverse, b_inverse
        )

    return program
```

time: 401 us -> 177 us (0.44)
  Pallas kernels: 0 us -> 177 us
  waiting for transfers between devices: 164 us -> 0 us
  blocking collectives: 81 us -> 0 us
  other arithmetic: 74 us -> 0 us
  local copies, waits for them, and re-layouts: 32.6 us -> 0 us
  matrix products: 30.5 us -> 0 us
  between operations: 13.5 us -> 0.01 us
  starting transfers between devices: 5.55 us -> 0 us
    pallas_call x0 -> x3, Pallas kernels: none -> 177 us  [the longest x1 163 us: fused(): pl.pallas_call(functools.partial(kernel, groups, width, tile, side), out_...]
    all_gather x2 -> x0, waiting for transfers between devices: 89.2 us -> none  [the longest x1 85.2 us: local(): lax.all_gather(right_half, 'shard', axis=0, tiled=True)]
    all_to_all x1 -> x0, blocking collectives: 81 us -> none  [local(): lax.all_to_all(outgoing, 'dp', split_axis=0, concat_axis=1, tiled=True)]
    all_to_all x1 -> x0, waiting for transfers between devices: 73.9 us -> none  [local(): lax.all_to_all(result_rows[None, :, :], 'dp', split_axis=1, concat_axis=0...]
    unnamed x1 -> x0, other arithmetic: 70 us -> none
    dot_general x3 -> x0, matrix products: 30.5 us -> none  [the longest x1 14.4 us: local(): jnp.dot(columns, lax.all_gather(right_half, 'shard', axis=0, tiled=True),...]
    unnamed x10 -> x0, local copies, waits for them, and re-layouts: 16.9 us -> none
    broadcast_in_dim x1 -> x0, local copies, waits for them, and re-layouts: 10.2 us -> none  [local(): result_rows[None, :, :]]
  transfers between devices with their start and end apart: 3 -> 0, of which waited for: 3 -> 0; matrix products, arithmetic and copies ran while one was open for 1% -> 0% of each run, Pallas kernels for 0% -> 0%
where the time goes in v1:
time: 177 us
  Pallas kernels  177 us (100%)
    pallas_call x1, Pallas kernels, fused(): pl.pallas_call(functools.partial(kernel, groups, width, tile, side), out_...  163 us
    pallas_call x2, Pallas kernels, permute(): pl.pallas_call(copy_block, out_shape=jax.ShapeDtypeStruct(array.shape, ar...  13.7 us

profile of v1, /device:TPU:0, one launch (start us, length us, event | category | flops | bytes accessed | tf_op | source)
XLA Modules:
  0.0 176.7 jit_solution(15055400387544276772)
XLA Ops:
  0.0 6.8 %shard_map.46.g_ref = bf16[8,80,2560]{2,1,0:T(8,128)(2,1)} custom-call(s32[8]{0:T(128)} %owner_ref.3, bf16[8,80,2560]{2,1,0:T(8,128)(2,1)} %in_ref.1), custom_call_target="tpu_custom_call" | custom-call | bytes 6553600 | tf_op jit(solution)/shard_map/pallas_call | solution.py:43
  6.8 163.0 %shard_map.47.in_ref = bf16[8,80,2560]{2,1,0:T(8,128)(2,1)} custom-call(bf16[8,80,2560]{2,1,0:T(8,128)(2,1)} %shard_map.46.g_ref, bf16[640,2560]{1,0:T(8,128)(2,1)} %bitcast.2, bf16[640,2560]{1,0:T(8,128)(2,1)} %bitcast.3), custom_call_target="tpu_custom_call" | custom-call | flops 16777216000 | bytes 13107200 | tf_op jit(solution)/shard_map/pallas_call | solution.py:243
  169.9 6.9 %shard_map.48 = bf16[8,80,2560]{2,1,0:T(8,128)(2,1)} custom-call(s32[8]{0:T(128)} %owner_ref.3, bf16[8,80,2560]{2,1,0:T(8,128)(2,1)} %shard_map.47.in_ref), custom_call_target="tpu_custom_call" | custom-call | bytes 6553600 | tf_op jit(solution)/shard_map/pallas_call | solution.py:43

commit v2 on v1

--- a/solution.py
+++ b/solution.py
@@ -32,23 +32,27 @@
     return jnp.take(returned, owner, axis=0)
 
 
-def copy_block(owner_ref, in_ref, out_ref):
-    out_ref[...] = in_ref[...]
+def move(scatter, owner_ref, in_ref, out_ref, sems):
+    layers = in_ref.shape[0]
+    copies = []
+    for l in range(layers):
+        slot = owner_ref[l]
+        src, dst = (l, slot) if scatter else (slot, l)
+        copies.append(pltpu.make_async_copy(in_ref.at[src], out_ref.at[dst], sems.at[l]))
+        copies[-1].start()
+    for copy in copies:
+        copy.wait()
 
 
 def permute(owner, array, scatter):
     layers, rows, dim = array.shape
-    plain = lambda l, owner_ref: (l, 0, 0)
-    moved = lambda l, owner_ref: (owner_ref[l], 0, 0)
+    anywhere = pl.BlockSpec(memory_space=pl.ANY)
     return pl.pallas_call(
-        copy_block,
+        functools.partial(move, scatter),
         out_shape=jax.ShapeDtypeStruct(array.shape, array.dtype),
-        grid_spec=pltpu.PrefetchScalarGridSpec(
-            num_scalar_prefetch=1,
-            grid=(layers,),
-            in_specs=[pl.BlockSpec((1, rows, dim), plain if scatter else moved)],
-            out_specs=pl.BlockSpec((1, rows, dim), moved if scatter else plain),
-        ),
+        in_specs=[pl.BlockSpec(memory_space=pltpu.SMEM), anywhere],
+        out_specs=anywhere,
+        scratch_shapes=[pltpu.SemaphoreType.DMA((layers,))],
         cost_estimate=pl.CostEstimate(flops=0, bytes_accessed=4 * layers * rows * dim, transcendentals=0),
     )(owner, array)
 
@@ -189,28 +193,53 @@
         copy.wait_recv()
 
     chunks = dim // width
-
-    def give(j, carry):
-        psend[j] = dot(ap[...], rbuf[:, rows_of(j, width)]).astype(BF16)
-        remote(psend.at[j], prec.at[j], p_send.at[j], p_recv.at[j], (d, across)).start()
-        return carry
-
-    lax.fori_loop(0, chunks, give, 0)
-
-    def finish(j, carry):
-        columns = rows_of(j, width)
-        mine = dot(abuf[:, own_half], rbuf[:, columns])
-        remote(psend.at[j], prec.at[j], p_send.at[j], p_recv.at[j], (d, across)).wait_recv()
-        obuf[:, columns] = (mine + prec[j].astype(F32)).astype(BF16)
-        for k in (4, 5, 6, 7, 2, 3, 1):
-            peer = flip(d, k)
-            remote(
-                obuf.at[rows_of(peer, rows), columns], o_ref.at[d, :, columns],
-                o_send.at[k], o_recv.at[k], (peer, s),
-            ).start()
-        return carry
-
-    lax.fori_loop(0, chunks, finish, 0)
+    pieces = 2 * chunks
+    z_half = d // (groups // 2)
+    piece_rows = quarter // 2
+
+    def place(i):
+        late = i // chunks
+        target = late * z_half + (1 - late) * (1 - z_half)
+        return late, target, rows_of(target, piece_rows), rows_of(i - late * chunks, width)
+
+    def partial(i):
+        return remote(psend.at[i], prec.at[i], p_send.at[i], p_recv.at[i], (d, across))
+
+    def give(i):
+        _, _, here, columns = place(i)
+        psend[i] = dot(ap[here, :], rbuf[:, columns]).astype(BF16)
+        partial(i).start()
+
+    def finish(i, carry):
+        late, target, here, columns = place(i)
+        mine = dot(abuf[here, own_half], rbuf[:, columns])
+        partial(i).wait_recv()
+        obuf[here, columns] = (mine + prec[i].astype(F32)).astype(BF16)
+        for q in range(groups // 2):
+            peer = target * (groups // 2) + lax.rem(flip(d, q), groups // 2)
+            k = (1 - late) * (groups // 2) + q
+
+            def send(peer=peer, k=k):
+                remote(
+                    obuf.at[rows_of(peer, rows), columns], o_ref.at[d, :, columns],
+                    o_send.at[k], o_recv.at[k], (peer, s),
+                ).start()
+
+            if q == 0:
+                pl.when(late == 0)(send)
+            else:
+                send()
+
+        @pl.when(i + lead < pieces)
+        def _():
+            give(i + lead)
+
+        return carry
+
+    lead = 4
+    for i in range(lead):
+        give(i)
+    lax.fori_loop(0, pieces, finish, 0)
     o_own = pltpu.make_async_copy(obuf.at[rows_of(d, rows)], o_ref.at[d], local_sem.at[3])
     o_own.start()
 
@@ -219,11 +248,11 @@
     for copy in (b_across, b_sib, a_sib, relay, *r_copies):
         copy.wait_send()
 
-    def sent(j, carry):
-        remote(psend.at[j], prec.at[j], p_send.at[j], p_recv.at[j], (d, across)).wait_send()
-        return carry
-
-    lax.fori_loop(0, chunks, sent, 0)
+    def sent(i, carry):
+        partial(i).wait_send()
+        return carry
+
+    lax.fori_loop(0, pieces, sent, 0)
     o_own.wait()
     for k in range(1, groups):
         peer = flip(d, k)
@@ -252,14 +281,14 @@
             pltpu.VMEM((quarter, quarter), BF16),
             pltpu.VMEM((quarter, half), BF16),
             pltpu.VMEM((half, dim), BF16),
-            pltpu.VMEM((chunks, quarter, width), BF16),
-            pltpu.VMEM((chunks, quarter, width), BF16),
+            pltpu.VMEM((2 * chunks, quarter // 2, width), BF16),
+            pltpu.VMEM((2 * chunks, quarter // 2, width), BF16),
             pltpu.VMEM((quarter, dim), BF16),
             dma((4,)),
             dma((groups,)), dma((groups,)),
             dma((4,)), dma((4,)),
             dma((groups // 2,)), dma((groups // 2,)),
-            dma((chunks,)), dma((chunks,)),
+            dma((2 * chunks,)), dma((2 * chunks,)),
             dma((groups,)), dma((groups,)),
         ],
         compiler_params=pltpu.CompilerParams(

time: 177 us -> 398 us (2.25)
  Pallas kernels: 177 us -> 398 us
    pallas_call x2, Pallas kernels: 13.7 us -> 202 us  [permute(): pl.pallas_call(functools.partial(move, scatter), out_shape=jax.ShapeDtype...]
    pallas_call x1, Pallas kernels: 163 us -> 196 us  [fused(): pl.pallas_call(functools.partial(kernel, groups, width, tile, side), out_...]
where the time goes in v2:
time: 398 us
  Pallas kernels  398 us (100%)
    pallas_call x2, Pallas kernels, permute(): pl.pallas_call(functools.partial(move, scatter), out_shape=jax.ShapeDtype...  202 us
    pallas_call x1, Pallas kernels, fused(): pl.pallas_call(functools.partial(kernel, groups, width, tile, side), out_...  196 us

profile of v2, /device:TPU:0, one launch (start us, length us, event | category | flops | bytes accessed | tf_op | source)
XLA Modules:
  0.0 398.3 jit_solution(2348438149534690312)
XLA Ops:
  0.0 101.1 %shard_map.46.g_ref = bf16[8,80,2560]{2,1,0:T(8,128)(2,1)} custom-call(s32[8]{0:T(128)} %owner_ref.3, bf16[8,80,2560]{2,1,0:T(8,128)(2,1)} %in_ref.1), custom_call_target="tpu_custom_call" | custom-call | bytes 6553600 | tf_op jit(solution)/shard_map/pallas_call | solution.py:50
  101.1 196.1 %shard_map.47.in_ref = bf16[8,80,2560]{2,1,0:T(8,128)(2,1)} custom-call(bf16[8,80,2560]{2,1,0:T(8,128)(2,1)} %shard_map.46.g_ref, bf16[640,2560]{1,0:T(8,128)(2,1)} %bitcast.2, bf16[640,2560]{1,0:T(8,128)(2,1)} %bitcast.3), custom_call_target="tpu_custom_call" | custom-call | flops 16777216000 | bytes 13107200 | tf_op jit(solution)/shard_map/pallas_call | solution.py:272
  297.2 101.1 %shard_map.48 = bf16[8,80,2560]{2,1,0:T(8,128)(2,1)} custom-call(s32[8]{0:T(128)} %owner_ref.3, bf16[8,80,2560]{2,1,0:T(8,128)(2,1)} %shard_map.47.in_ref), custom_call_target="tpu_custom_call" | custom-call | bytes 6553600 | tf_op jit(solution)/shard_map/pallas_call | solution.py:50

commit v3 on v2

--- a/solution.py
+++ b/solution.py
@@ -32,27 +32,34 @@
     return jnp.take(returned, owner, axis=0)
 
 
-def move(scatter, owner_ref, in_ref, out_ref, sems):
+def collect(owner_ref, in_ref, out_ref, held, in_sems, out_sems):
     layers = in_ref.shape[0]
-    copies = []
+    loads = []
     for l in range(layers):
-        slot = owner_ref[l]
-        src, dst = (l, slot) if scatter else (slot, l)
-        copies.append(pltpu.make_async_copy(in_ref.at[src], out_ref.at[dst], sems.at[l]))
-        copies[-1].start()
-    for copy in copies:
-        copy.wait()
-
-
-def permute(owner, array, scatter):
+        loads.append(pltpu.make_async_copy(in_ref.at[owner_ref[l]], held.at[l], in_sems.at[l]))
+        loads[-1].start()
+    stores = []
+    for l in range(layers):
+        loads[l].wait()
+        stores.append(pltpu.make_async_copy(held.at[l], out_ref.at[l], out_sems.at[l]))
+        stores[-1].start()
+    for store in stores:
+        store.wait()
+
+
+def to_layers(owner, array):
     layers, rows, dim = array.shape
     anywhere = pl.BlockSpec(memory_space=pl.ANY)
     return pl.pallas_call(
-        functools.partial(move, scatter),
+        collect,
         out_shape=jax.ShapeDtypeStruct(array.shape, array.dtype),
         in_specs=[pl.BlockSpec(memory_space=pltpu.SMEM), anywhere],
         out_specs=anywhere,
-        scratch_shapes=[pltpu.SemaphoreType.DMA((layers,))],
+        scratch_shapes=[
+            pltpu.VMEM(array.shape, array.dtype),
+            pltpu.SemaphoreType.DMA((layers,)),
+            pltpu.SemaphoreType.DMA((layers,)),
+        ],
         cost_estimate=pl.CostEstimate(flops=0, bytes_accessed=4 * layers * rows * dim, transcendentals=0),
     )(owner, array)
 
@@ -72,8 +79,8 @@
 
 def kernel(
     groups, width, tile, side,
-    g_ref, a_ref, b_ref, o_ref,
-    gbuf, bfull, abuf, asib, ap, rbuf, psend, prec, obuf,
+    owner_ref, g_ref, a_ref, b_ref, o_ref,
+    gsend, gbuf, acc, bfull, abuf, asib, ap, rbuf, psend, prec, obuf,
     local_sem, g_send, g_recv, b_send, b_recv, r_send, r_recv, p_send, p_recv, o_send, o_recv,
 ):
     _, rows, dim = g_ref.shape
@@ -100,13 +107,6 @@
         pl.semaphore_signal(barrier, inc=1, device_id=(d, other), device_id_type=MESH)
     pl.semaphore_wait(barrier, groups + 1)
 
-    g_copies = {}
-    for k in (4, 5, 6, 7, 2, 3, 1):
-        peer = flip(d, k)
-        g_copies[k] = remote(
-            g_ref.at[peer], gbuf.at[rows_of(d, rows)], g_send.at[k], g_recv.at[k], (peer, s)
-        )
-        g_copies[k].start()
     own_half = rows_of(y, half)
     other_half = rows_of(1 - y, half)
     b_across = remote(
@@ -121,8 +121,37 @@
     a_own.start()
     b_own = pltpu.make_async_copy(b_ref, bfull.at[rows_of(s, quarter)], local_sem.at[1])
     b_own.start()
-    g_own = pltpu.make_async_copy(g_ref.at[d], gbuf.at[rows_of(d, rows)], local_sem.at[2])
-    g_own.start()
+
+    def layer_of(slot):
+        found = 0
+        for l in range(groups):
+            found = jnp.where(owner_ref[l] == slot, l, found)
+        return found
+
+    parts = (s, sib, across, across_sib)
+    order = (4, 2, 5, 3, 6, 1, 7)
+
+    def gradient_copy(part, k):
+        peer, columns = flip(d, k), rows_of(parts[part], quarter)
+        return remote(
+            gsend.at[k, :, columns], gbuf.at[rows_of(d, rows), columns],
+            g_send.at[part, k], g_recv.at[part, k], (peer, s),
+        )
+
+    def arrival(part, k):
+        peer, columns = flip(d, k), rows_of(parts[part], quarter)
+        return remote(
+            gsend.at[k, :, columns], gbuf.at[rows_of(peer, rows), columns],
+            g_send.at[part, k], g_recv.at[part, k], (peer, s),
+        )
+
+    for k in order:
+        gsend[k] = g_ref[layer_of(flip(d, k))]
+        gradient_copy(0, k).start()
+    for part in range(1, 4):
+        for k in order:
+            gradient_copy(part, k).start()
+    gbuf[rows_of(d, rows), :] = g_ref[layer_of(d)]
 
     a_own.wait()
     per = quarter // side
@@ -162,35 +191,41 @@
 
     lax.fori_loop(0, wide * wide, turn_b, 0)
 
+    def add_part(part):
+        for k in order:
+            arrival(part, k).wait_recv()
+        depth = rows_of(parts[part], quarter)
+
+        def product(t, carry):
+            columns = rows_of(t, tile)
+            term = dot(gbuf[:, depth], bfull[depth, columns])
+            if part == 0:
+                acc[:, columns] = term
+            elif part < 3:
+                acc[:, columns] += term
+            else:
+                rbuf[here, columns] = (acc[:, columns] + term).astype(BF16)
+                half_copy(t).start()
+            return carry
+
+        lax.fori_loop(0, dim // tile, product, 0)
+
+    here = rows_of(c, quarter)
+
+    def half_copy(t):
+        block = rbuf.at[here, rows_of(t, tile)]
+        return remote(block, block, r_send.at[t], r_recv.at[t], (d, sib))
+
+    add_part(0)
+    add_part(1)
+
     arrived = bfull.at[rows_of(across, quarter), other_half]
     remote(arrived, arrived, b_send.at[0], b_recv.at[0], (d, across)).wait_recv()
     relay = remote(arrived, arrived, b_send.at[3], b_recv.at[3], (d, sib))
     relay.start()
+    add_part(2)
     relay.wait_recv()
-
-    pair = 2 * rows
-    r_copies = []
-    for step in range(groups // 2):
-        first = flip(d // 2, step)
-        if step == 0:
-            g_own.wait()
-            g_copies[1].wait_recv()
-        else:
-            g_copies[2 * step].wait_recv()
-            g_copies[2 * step + 1].wait_recv()
-        here = pl.ds(pl.multiple_of(c * quarter + first * pair, pair), pair)
-
-        def product(t, carry, first=first, here=here):
-            columns = rows_of(t, tile)
-            rbuf[here, columns] = dot(gbuf[rows_of(first, pair), :], bfull[:, columns]).astype(BF16)
-            return carry
-
-        lax.fori_loop(0, dim // tile, product, 0)
-        copy = remote(rbuf.at[here], rbuf.at[here], r_send.at[step], r_recv.at[step], (d, sib))
-        copy.start()
-        r_copies.append(copy)
-    for copy in r_copies:
-        copy.wait_recv()
+    add_part(3)
 
     chunks = dim // width
     pieces = 2 * chunks
@@ -198,15 +233,22 @@
     piece_rows = quarter // 2
 
     def place(i):
-        late = i // chunks
+        late = lax.rem(i, 2)
         target = late * z_half + (1 - late) * (1 - z_half)
-        return late, target, rows_of(target, piece_rows), rows_of(i - late * chunks, width)
+        return late, target, rows_of(target, piece_rows), rows_of(i // 2, width)
 
     def partial(i):
         return remote(psend.at[i], prec.at[i], p_send.at[i], p_recv.at[i], (d, across))
 
+    per_tile = 2 * tile // width
+
     def give(i):
         _, _, here, columns = place(i)
+
+        @pl.when(lax.rem(i, per_tile) == 0)
+        def _():
+            half_copy(i // per_tile).wait_recv()
+
         psend[i] = dot(ap[here, :], rbuf[:, columns]).astype(BF16)
         partial(i).start()
 
@@ -243,9 +285,12 @@
     o_own = pltpu.make_async_copy(obuf.at[rows_of(d, rows)], o_ref.at[d], local_sem.at[3])
     o_own.start()
 
-    for k in range(1, groups):
-        g_copies[k].wait_send()
-    for copy in (b_across, b_sib, a_sib, relay, *r_copies):
+    for part in range(4):
+        for k in order:
+            gradient_copy(part, k).wait_send()
+    for t in range(dim // tile):
+        half_copy(t).wait_send()
+    for copy in (b_across, b_sib, a_sib, relay):
         copy.wait_send()
 
     def sent(i, carry):
@@ -266,16 +311,17 @@
     quarter, half = dim // 4, dim // 2
     width, tile, side = 256, 512, 128
     chunks = dim // width
-    outgoing = permute(owner, gradient, True)
     anywhere = pl.BlockSpec(memory_space=pl.ANY)
     dma = pltpu.SemaphoreType.DMA
     returned = pl.pallas_call(
         functools.partial(kernel, groups, width, tile, side),
         out_shape=jax.ShapeDtypeStruct(gradient.shape, BF16),
-        in_specs=[anywhere] * 3,
+        in_specs=[pl.BlockSpec(memory_space=pltpu.SMEM), pl.BlockSpec(memory_space=pltpu.VMEM), anywhere, anywhere],
         out_specs=anywhere,
         scratch_shapes=[
+            pltpu.VMEM(gradient.shape, BF16),
             pltpu.VMEM((quarter, dim), BF16),
+            pltpu.VMEM((quarter, dim), F32),
             pltpu.VMEM((dim, dim), BF16),
             pltpu.VMEM((quarter, dim), BF16),
             pltpu.VMEM((quarter, quarter), BF16),
@@ -285,20 +331,20 @@
             pltpu.VMEM((2 * chunks, quarter // 2, width), BF16),
             pltpu.VMEM((quarter, dim), BF16),
             dma((4,)),
-            dma((groups,)), dma((groups,)),
+            dma((4, groups)), dma((4, groups)),
             dma((4,)), dma((4,)),
-            dma((groups // 2,)), dma((groups // 2,)),
+            dma((dim // tile,)), dma((dim // tile,)),
             dma((2 * chunks,)), dma((2 * chunks,)),
             dma((groups,)), dma((groups,)),
         ],
         compiler_params=pltpu.CompilerParams(
-            collective_id=0, has_side_effects=True, vmem_limit_bytes=56 * 1024 * 1024
+            collective_id=0, has_side_effects=True, vmem_limit_bytes=60 * 1024 * 1024
         ),
         cost_estimate=pl.CostEstimate(
             flops=4 * quarter * dim * dim, bytes_accessed=8 * quarter * dim, transcendentals=0
         ),
-    )(outgoing, a_inverse[0], b_inverse[0])
-    return permute(owner, returned, False)
+    )(owner, gradient, a_inverse[0], b_inverse[0])
+    return to_layers(owner, returned)
 
 
 def solution(mesh):

time: 398 us -> 166 us (0.42)
  Pallas kernels: 398 us -> 166 us
    pallas_call x2 -> x1, Pallas kernels: 202 us -> 3.51 us  [to_layers(): pl.pallas_call(collect, out_shape=jax.ShapeDtypeStruct(array.shape, array...]
    pallas_call x1, Pallas kernels: 196 us -> 162 us  [fused(): pl.pallas_call(functools.partial(kernel, groups, width, tile, side), out_...]
where the time goes in v3:
time: 166 us
  Pallas kernels  166 us (100%)
    pallas_call x1, Pallas kernels, fused(): pl.pallas_call(functools.partial(kernel, groups, width, tile, side), out_...  162 us
    pallas_call x1, Pallas kernels, to_layers(): pl.pallas_call(collect, out_shape=jax.ShapeDtypeStruct(array.shape, array...  3.51 us

profile of v3, /device:TPU:0, one launch (start us, length us, event | category | flops | bytes accessed | tf_op | source)
XLA Modules:
  0.0 165.9 jit_solution(9415476465587041380)
XLA Ops:
  0.0 162.4 %shard_map.46.in_ref = bf16[8,80,2560]{2,1,0:T(8,128)(2,1)} custom-call(s32[8]{0:T(128)} %owner_ref.3, bf16[8,80,2560]{2,1,0:T(8,128)(2,1)} %g_ref.1, bf16[640,2560]{1,0:T(8,128)(2,1)} %bitcast.2, bf16[640,2560]{1,0:T(8,128)(2,1)} %bitcast.3), custom_call_target="tpu_custom_call" | custom-call | flops 16777216000 | bytes 13107200 | tf_op jit(solution)/shard_map/pallas_call | solution.py:316
  162.4 3.5 %shard_map.47 = bf16[8,80,2560]{2,1,0:T(8,128)(2,1)} custom-call(s32[8]{0:T(128)} %owner_ref.3, bf16[8,80,2560]{2,1,0:T(8,128)(2,1)} %shard_map.46.in_ref), custom_call_target="tpu_custom_call" | custom-call | bytes 6553600 | tf_op jit(solution)/shard_map/pallas_call | solution.py:53

commit v4 on v3

--- a/solution.py
+++ b/solution.py
@@ -80,7 +80,7 @@
 def kernel(
     groups, width, tile, side,
     owner_ref, g_ref, a_ref, b_ref, o_ref,
-    gsend, gbuf, acc, bfull, abuf, asib, ap, rbuf, psend, prec, obuf,
+    gin, gsend, gbuf, acc, bfull, abuf, asib, ap, rbuf, psend, prec, obuf,
     local_sem, g_send, g_recv, b_send, b_recv, r_send, r_recv, p_send, p_recv, o_send, o_recv,
 ):
     _, rows, dim = g_ref.shape
@@ -100,6 +100,13 @@
             src_ref=src, dst_ref=dst, send_sem=send, recv_sem=recv, device_id=device, device_id_type=MESH
         )
 
+    g_in = pltpu.make_async_copy(g_ref, gin, local_sem.at[2])
+    g_in.start()
+    a_own = pltpu.make_async_copy(a_ref, abuf, local_sem.at[0])
+    a_own.start()
+    b_own = pltpu.make_async_copy(b_ref, bfull.at[rows_of(s, quarter)], local_sem.at[1])
+    b_own.start()
+
     barrier = pltpu.get_barrier_semaphore()
     for k in range(1, groups):
         pl.semaphore_signal(barrier, inc=1, device_id=(flip(d, k), s), device_id_type=MESH)
@@ -109,6 +116,33 @@
 
     own_half = rows_of(y, half)
     other_half = rows_of(1 - y, half)
+    def layer_of(slot):
+        found = 0
+        for l in range(groups):
+            found = jnp.where(owner_ref[l] == slot, l, found)
+        return found
+
+    parts = (s, sib, across, across_sib)
+    order = (4, 2, 5, 3, 6, 1, 7)
+
+    def gradient_copy(part, k):
+        peer, columns = flip(d, k), rows_of(parts[part], quarter)
+        return remote(
+            gsend.at[k, :, columns], gbuf.at[rows_of(d, rows), columns],
+            g_send.at[part, k], g_recv.at[part, k], (peer, s),
+        )
+
+    def arrival(part, k):
+        peer, columns = flip(d, k), rows_of(parts[part], quarter)
+        return remote(
+            gsend.at[k, :, columns], gbuf.at[rows_of(peer, rows), columns],
+            g_send.at[part, k], g_recv.at[part, k], (peer, s),
+        )
+
+    g_in.wait()
+    for k in order:
+        gsend[k] = gin[layer_of(flip(d, k))]
+        gradient_copy(0, k).start()
     b_across = remote(
         b_ref.at[:, own_half], bfull.at[rows_of(s, quarter), own_half], b_send.at[0], b_recv.at[0], (d, across)
     )
@@ -117,41 +151,10 @@
     b_sib.start()
     a_sib = remote(a_ref.at[:, rows_of(across_sib, quarter)], asib, b_send.at[2], b_recv.at[2], (d, sib))
     a_sib.start()
-    a_own = pltpu.make_async_copy(a_ref, abuf, local_sem.at[0])
-    a_own.start()
-    b_own = pltpu.make_async_copy(b_ref, bfull.at[rows_of(s, quarter)], local_sem.at[1])
-    b_own.start()
-
-    def layer_of(slot):
-        found = 0
-        for l in range(groups):
-            found = jnp.where(owner_ref[l] == slot, l, found)
-        return found
-
-    parts = (s, sib, across, across_sib)
-    order = (4, 2, 5, 3, 6, 1, 7)
-
-    def gradient_copy(part, k):
-        peer, columns = flip(d, k), rows_of(parts[part], quarter)
-        return remote(
-            gsend.at[k, :, columns], gbuf.at[rows_of(d, rows), columns],
-            g_send.at[part, k], g_recv.at[part, k], (peer, s),
-        )
-
-    def arrival(part, k):
-        peer, columns = flip(d, k), rows_of(parts[part], quarter)
-        return remote(
-            gsend.at[k, :, columns], gbuf.at[rows_of(peer, rows), columns],
-            g_send.at[part, k], g_recv.at[part, k], (peer, s),
-        )
-
-    for k in order:
-        gsend[k] = g_ref[layer_of(flip(d, k))]
-        gradient_copy(0, k).start()
     for part in range(1, 4):
         for k in order:
             gradient_copy(part, k).start()
-    gbuf[rows_of(d, rows), :] = g_ref[layer_of(d)]
+    gbuf[rows_of(d, rows), :] = gin[layer_of(d)]
 
     a_own.wait()
     per = quarter // side
@@ -309,16 +312,17 @@
 def fused(gradient, owner, a_inverse, b_inverse):
     groups, rows, dim = gradient.shape
     quarter, half = dim // 4, dim // 2
-    width, tile, side = 256, 512, 128
+    width, tile, side = 256, 256, 128
     chunks = dim // width
     anywhere = pl.BlockSpec(memory_space=pl.ANY)
     dma = pltpu.SemaphoreType.DMA
     returned = pl.pallas_call(
         functools.partial(kernel, groups, width, tile, side),
         out_shape=jax.ShapeDtypeStruct(gradient.shape, BF16),
-        in_specs=[pl.BlockSpec(memory_space=pltpu.SMEM), pl.BlockSpec(memory_space=pltpu.VMEM), anywhere, anywhere],
+        in_specs=[pl.BlockSpec(memory_space=pltpu.SMEM), anywhere, anywhere, anywhere],
         out_specs=anywhere,
         scratch_shapes=[
+            pltpu.VMEM(gradient.shape, BF16),
             pltpu.VMEM(gradient.shape, BF16),
             pltpu.VMEM((quarter, dim), BF16),
             pltpu.VMEM((quarter, dim), F32),

time: 166 us -> 165 us (level)
  no operation moved by 1% of the time
where the time goes in v4:
time: 165 us
  Pallas kernels  165 us (100%)
    pallas_call x1, Pallas kernels, fused(): pl.pallas_call(functools.partial(kernel, groups, width, tile, side), out_...  161 us
    pallas_call x1, Pallas kernels, to_layers(): pl.pallas_call(collect, out_shape=jax.ShapeDtypeStruct(array.shape, array...  3.51 us

profile of v4, /device:TPU:0, one launch (start us, length us, event | category | flops | bytes accessed | tf_op | source)
XLA Modules:
  0.0 164.6 jit_solution(4728257600482418320)
XLA Ops:
  0.0 161.0 %shard_map.46.in_ref = bf16[8,80,2560]{2,1,0:T(8,128)(2,1)} custom-call(s32[8]{0:T(128)} %owner_ref.3, bf16[8,80,2560]{2,1,0:T(8,128)(2,1)} %g_ref.1, bf16[640,2560]{1,0:T(8,128)(2,1)} %bitcast.2, bf16[640,2560]{1,0:T(8,128)(2,1)} %bitcast.3), custom_call_target="tpu_custom_call" | custom-call | flops 16777216000 | bytes 13107200 | tf_op jit(solution)/shard_map/pallas_call | solution.py:319
  161.0 3.5 %shard_map.47 = bf16[8,80,2560]{2,1,0:T(8,128)(2,1)} custom-call(s32[8]{0:T(128)} %owner_ref.3, bf16[8,80,2560]{2,1,0:T(8,128)(2,1)} %shard_map.46.in_ref), custom_call_target="tpu_custom_call" | custom-call | bytes 6553600 | tf_op jit(solution)/shard_map/pallas_call | solution.py:53

commit v5 on v4

--- a/solution.py
+++ b/solution.py
@@ -236,7 +236,7 @@
     piece_rows = quarter // 2
 
     def place(i):
-        late = lax.rem(i, 2)
+        late = lax.rem(i + c, 2)
         target = late * z_half + (1 - late) * (1 - z_half)
         return late, target, rows_of(target, piece_rows), rows_of(i // 2, width)
 

time: 165 us -> 165 us (level)
  no operation moved by 1% of the time
where the time goes in v5:
time: 165 us
  Pallas kernels  165 us (100%)
    pallas_call x1, Pallas kernels, fused(): pl.pallas_call(functools.partial(kernel, groups, width, tile, side), out_...  161 us
    pallas_call x1, Pallas kernels, to_layers(): pl.pallas_call(collect, out_shape=jax.ShapeDtypeStruct(array.shape, array...  3.51 us

profile of v5, /device:TPU:0, one launch (start us, length us, event | category | flops | bytes accessed | tf_op | source)
XLA Modules:
  0.0 164.7 jit_solution(322037787946563430)
XLA Ops:
  0.0 161.2 %shard_map.46.in_ref = bf16[8,80,2560]{2,1,0:T(8,128)(2,1)} custom-call(s32[8]{0:T(128)} %owner_ref.3, bf16[8,80,2560]{2,1,0:T(8,128)(2,1)} %g_ref.1, bf16[640,2560]{1,0:T(8,128)(2,1)} %bitcast.2, bf16[640,2560]{1,0:T(8,128)(2,1)} %bitcast.3), custom_call_target="tpu_custom_call" | custom-call | flops 16777216000 | bytes 13107200 | tf_op jit(solution)/shard_map/pallas_call | solution.py:319
  161.2 3.5 %shard_map.47 = bf16[8,80,2560]{2,1,0:T(8,128)(2,1)} custom-call(s32[8]{0:T(128)} %owner_ref.3, bf16[8,80,2560]{2,1,0:T(8,128)(2,1)} %shard_map.46.in_ref), custom_call_target="tpu_custom_call" | custom-call | bytes 6553600 | tf_op jit(solution)/shard_map/pallas_call | solution.py:53

commit v6 on v4

--- a/solution.py
+++ b/solution.py
@@ -194,8 +194,8 @@
 
     lax.fori_loop(0, wide * wide, turn_b, 0)
 
-    def add_part(part):
-        for k in order:
+    def add_part(part, first=0, last=dim // tile):
+        for k in order if first == 0 else ():
             arrival(part, k).wait_recv()
         depth = rows_of(parts[part], quarter)
 
@@ -211,7 +211,7 @@
                 half_copy(t).start()
             return carry
 
-        lax.fori_loop(0, dim // tile, product, 0)
+        lax.fori_loop(first, last, product, 0)
 
     here = rows_of(c, quarter)
 
@@ -228,7 +228,8 @@
     relay.start()
     add_part(2)
     relay.wait_recv()
-    add_part(3)
+    early = 4
+    add_part(3, 0, early)
 
     chunks = dim // width
     pieces = 2 * chunks
@@ -284,6 +285,7 @@
     lead = 4
     for i in range(lead):
         give(i)
+    add_part(3, early)
     lax.fori_loop(0, pieces, finish, 0)
     o_own = pltpu.make_async_copy(obuf.at[rows_of(d, rows)], o_ref.at[d], local_sem.at[3])
     o_own.start()

time: 165 us -> 163 us (0.988)
  Pallas kernels: 165 us -> 163 us
where the time goes in v6:
time: 163 us
  Pallas kernels  163 us (100%)
    pallas_call x1, Pallas kernels, fused(): pl.pallas_call(functools.partial(kernel, groups, width, tile, side), out_...  160 us
    pallas_call x1, Pallas kernels, to_layers(): pl.pallas_call(collect, out_shape=jax.ShapeDtypeStruct(array.shape, array...  3.51 us

profile of v6, /device:TPU:0, one launch (start us, length us, event | category | flops | bytes accessed | tf_op | source)
XLA Modules:
  0.0 163.1 jit_solution(13677558796268816107)
XLA Ops:
  0.0 159.5 %shard_map.46.in_ref = bf16[8,80,2560]{2,1,0:T(8,128)(2,1)} custom-call(s32[8]{0:T(128)} %owner_ref.3, bf16[8,80,2560]{2,1,0:T(8,128)(2,1)} %g_ref.1, bf16[640,2560]{1,0:T(8,128)(2,1)} %bitcast.2, bf16[640,2560]{1,0:T(8,128)(2,1)} %bitcast.3), custom_call_target="tpu_custom_call" | custom-call | flops 16777216000 | bytes 13107200 | tf_op jit(solution)/shard_map/pallas_call | solution.py:321
  159.5 3.5 %shard_map.47 = bf16[8,80,2560]{2,1,0:T(8,128)(2,1)} custom-call(s32[8]{0:T(128)} %owner_ref.3, bf16[8,80,2560]{2,1,0:T(8,128)(2,1)} %shard_map.46.in_ref), custom_call_target="tpu_custom_call" | custom-call | bytes 6553600 | tf_op jit(solution)/shard_map/pallas_call | solution.py:53
